TPU v7x, 256 devices: a whole 4x4x8 slice. The times are simulated.
256 devices in a mesh: ka: 16 (over x, y_lo, core), ga: 16 (over y_hi, z).
Axes of the slice: x: 4, y: 4 (y_hi: 2, y_lo: 2; y = y_hi * 2 + y_lo), z: 8, core: 2. Of those that a mesh axis runs over, the one named last changes fastest.
Arguments:
- orbitals: bfloat16 [16, 2, 16, 256, 256], P('ka', None, None, 'ga'), may hold values from -6 to 6
- kernel_spans: float32 [16, 256, 128], P(None, 'ga'), may hold values from 0.2 to 2
- span_owner: int32 [16, 256, 1], P(None, 'ga'), may hold values from 0 to 15; in each aligned block of 16 rows (0 to 15, 16 to 31, ..., all dimensions but the last counted through in order) at most 2 rows name the same one
- q_index: int32 [16, 16], replicated, may hold values from 0 to 15
Outputs:
- exchange_image: float32 [16, 2, 1, 256, 256], P('ka', None, None, 'ga')
- intersections: float32 [16, 2, 16, 1], P('ka')
Inputs may be any that keep to these rules, and one draw needn't show every extreme that they name: `span_owner`: in each aligned block of 16 rows (one momentum transfer, the rows of one device) no owner is named by more than 2 rows, a bound that some block reaches.
All inputs are finite; a program needn't handle non-finite values.
Results may differ from a plain program's by a relative error of at most 0.002.
Values may be sent and summed in bfloat16 or wider, within the bound.
A program may use at most 64 MiB of HBM per device.

v0:
```python
import math

import jax
import jax.numpy as jnp
from jax import lax
from jax.sharding import PartitionSpec as P

N1 = 256
N2 = 256
NI = 1
CAP = 2


def passed_along(shard, axis, by):
    peers = lax.axis_size(axis)
    return lax.ppermute(shard, axis, [(i, (i + by) % peers) for i in range(peers)])


def dft_tables(length):
    ramp = jnp.arange(length, dtype=jnp.int32)
    products = ramp[:, None] * ramp[None, :] % length
    angles = products.astype(jnp.float32) * (2.0 * math.pi / length)
    cosine = jnp.cos(angles).astype(jnp.bfloat16)
    sine_table = jnp.sin(angles).astype(jnp.bfloat16)
    forward = jnp.stack(
        [jnp.stack([cosine, -sine_table], 1), jnp.stack([sine_table, cosine], 1)], 0
    )
    inverse = jnp.stack(
        [jnp.stack([cosine, sine_table], 1), jnp.stack([-sine_table, cosine], 1)], 0
    )
    return (forward, inverse)


def pair_density(targets, partner):
    targets_wide = targets.astype(jnp.float32)
    partner_wide = partner.astype(jnp.float32)
    density_re = (
        targets_wide[0][:, None] * partner_wide[0][None]
        + targets_wide[1][:, None] * partner_wide[1][None]
    )
    density_im = (
        targets_wide[1][:, None] * partner_wide[0][None]
        - targets_wide[0][:, None] * partner_wide[1][None]
    )
    pairs = density_re.shape[0] * density_re.shape[1]
    shape_tail = density_re.shape[2:]
    return jnp.stack([density_re, density_im]).reshape((2, pairs) + shape_tail).astype(jnp.bfloat16)


def apply_pairs(potential, partner, targets_count):
    partner_wide = partner.astype(jnp.float32)
    potential = potential.reshape((2, targets_count, partner.shape[1]) + partner.shape[2:])
    image_re = jnp.sum(
        potential[0] * partner_wide[0][None] - potential[1] * partner_wide[1][None], axis=1
    )
    image_im = jnp.sum(
        potential[0] * partner_wide[1][None] + potential[1] * partner_wide[0][None], axis=1
    )
    return jnp.stack([image_re, image_im])


def plane_image(targets, partner, kernel_row, tables):
    forward_two, inverse_two, forward_one, inverse_one = tables
    density = pair_density(targets, partner)
    half_done = jnp.einsum(
        "cprx,cxog->oprg", density, forward_two, preferred_element_type=jnp.float32
    ).astype(jnp.bfloat16)
    spectrum = jnp.einsum(
        "cprg,croh->opgh", half_done, forward_one, preferred_element_type=jnp.float32
    )
    weighted = (spectrum * kernel_row).astype(jnp.bfloat16)
    returned = jnp.einsum(
        "cpgh,choa->opga", weighted, inverse_one, preferred_element_type=jnp.float32
    ).astype(jnp.bfloat16)
    potential = jnp.einsum(
        "cpga,cgob->opab", returned, inverse_two, preferred_element_type=jnp.float32
    ) * (1.0 / (N1 * N2))
    return apply_pairs(potential, partner, targets.shape[1])


def cycle_total(held, contrib, start, my_kpoint, cycle_length):

    def turn(turn_index, state):
        total, visitor = state
        total = total + contrib(visitor, (my_kpoint - turn_index) % cycle_length)
        visitor = passed_along(visitor, "ka", 1)
        return (total, visitor)

    total, visitor = lax.fori_loop(0, cycle_length - 1, turn, (start, held))
    return total + contrib(visitor, (my_kpoint - cycle_length + 1) % cycle_length)


def contract(left, right):
    return jnp.einsum("jrx,irx->ji", left, right, precision=lax.Precision.HIGHEST)


def per_device(orbitals, kernel_spans, span_owner, q_index):
    groups = lax.axis_size("ga")
    cycle_length = lax.axis_size("ka")
    my_kpoint = lax.axis_index("ka")
    orbital_block = orbitals[0]
    owner_ids = span_owner[:, :, 0]
    owner_hot = (
        owner_ids[:, :, None] == jnp.arange(groups, dtype=jnp.int32)[None, None, :]
    ).astype(jnp.int32)
    arrival = jnp.sum((jnp.cumsum(owner_hot, axis=1) - owner_hot) * owner_hot, axis=2)
    slot_index = owner_ids * CAP + arrival
    selector = (
        slot_index[:, None, :] == jnp.arange(groups * CAP, dtype=jnp.int32)[None, :, None]
    ).astype(jnp.float32)
    outgoing = jnp.einsum("qsi,qit->qst", selector, kernel_spans, precision=lax.Precision.HIGHEST)
    arrived = lax.all_to_all(
        outgoing.astype(jnp.bfloat16), "ga", split_axis=1, concat_axis=1, tiled=True
    ).astype(outgoing.dtype)
    kernel_block = arrived.reshape(arrived.shape[0], -1, N1)
    forward_two, inverse_two = dft_tables(N2)
    forward_one, inverse_one = dft_tables(N1)
    tables = (forward_two, inverse_two, forward_one, inverse_one)
    kernel_planes = lax.all_gather(
        kernel_block.astype(jnp.bfloat16), "ga", axis=1, tiled=True
    ).astype(kernel_block.dtype)
    held = lax.all_to_all(orbital_block, "ga", split_axis=1, concat_axis=2, tiled=True)
    targets = lax.all_gather(orbital_block[:, :NI], "ga", axis=2, tiled=True)

    def contrib(partner, partner_k):
        kernel_row = lax.dynamic_index_in_dim(
            kernel_planes, q_index[my_kpoint, partner_k], 0, keepdims=False
        )
        return plane_image(targets, partner, kernel_row, tables)

    start = jnp.zeros((2, NI, N1, N2), jnp.float32)
    total = cycle_total(held, contrib, start, my_kpoint, cycle_length)
    image = lax.psum_scatter(total, "ga", scatter_dimension=2, tiled=True) * (-1.0 / cycle_length)
    block_wide = orbital_block.astype(jnp.float32)
    intersection_re = contract(block_wide[0], image[0]) + contract(block_wide[1], image[1])
    intersection_im = contract(block_wide[0], image[1]) - contract(block_wide[1], image[0])
    summed = lax.psum(jnp.stack([intersection_re, intersection_im]), "ga")
    intersections = summed * (1.0 / math.sqrt(N1 * N2))
    return (image[None], intersections[None])


def solution(mesh):
    in_specs = (P("ka", None, None, "ga", None), P(None, "ga", None), P(None, "ga", None), P())
    out_specs = (P("ka", None, None, "ga", None), P("ka", None, None, None))
    return jax.shard_map(
        per_device, mesh=mesh, in_specs=in_specs, out_specs=out_specs, check_vma=False
    )
```

profile of v0, /device:TPU:6, one launch (start us, length us, event | category | flops | bytes accessed | tf_op | source)
XLA Modules:
  0.0 499.0 jit_solution(6698375011889880410)
XLA Ops:
  9.1 21.1 %all_to_all.17 = bf16[16,32,128]{2,0,1:T(8,128)(2,1)S(1)} all-to-all(bf16[16,32,128]{2,0,1:T(8,128)(2,1)S(1)} %copy.68), channel_id=1, replica_groups=mesh['ka'=16,'ga'=16] {'ga'}, dimensions={1} | all-to-all | bytes 262144 | tf_op jit(solution)/shard_map/all_to_all | solution.py:112
  31.0 1.7 copy.63
  32.6 3.5 all-to-all-start
  37.0 1.3 dynamic_slice.29
  43.2 42.9 %all_gather.6 = bf16[2,1,256,256]{3,2,1,0:T(8,128)(2,1)S(1)} all-gather(bf16[2,1,16,256]{3,2,1,0:T(8,128)(2,1)S(1)} %slice.152), channel_id=1, replica_groups=mesh['ka'=16,'ga'=16] {'ga'}, dimensions={2}, use_global_device_ids=true | all-gather | bytes 278528 | tf_op jit(solution)/shard_map/all_gather | solution.py:123
  88.3 23.6 %all-gather.2.cloned.1.call-done = bf16[16,256,256]{2,1,0:T(8,128)(2,1)} async-done(((bf16[16,16,256]{2,1,0:T(8,128)(2,1)}), bf16[16,256,256]{2,1,0:T(8,128)(2,1)}) %all-gather.2.cloned.1.call-update) | async-done | bytes 2097168 | tf_op jit(solution)/shard_map/all_gather | solution.py:119
  111.9 4.0 convert_element_type.225
  115.9 127.8 %while.20 = (s32[]{:T(128)}, f32[2,1,256,256]{3,2,1,0:T(8,128)S(1)}, bf16[2,1,256,256]{3,2,1,0:T(8,128)(2,1)}, bf16[2,1,256,256]{3,2,1,0:T(8,128)(2,1)S(1)}, bf1...) while((s32[]{:T(128)}, ...), condition=%wide.region_3.4_spmd.clone, body=%wide.region_2.3_spmd.clone.sunk | while | flops 539623424 | bytes 12321156 | solution.py:89
  116.9 1.3 dynamic_slice.38
  124.6 1.3 dynamic_slice.38
  155.6 1.6 collective-permute-start
  164.0 2.2 collective-permute-start
  173.0 2.2 collective-permute-start
  181.9 2.2 collective-permute-start
  190.9 2.2 collective-permute-start
  199.9 2.2 collective-permute-start
  208.8 2.2 collective-permute-start
  217.8 2.2 collective-permute-start
  226.8 2.2 collective-permute-start
  235.7 2.2 collective-permute-start
  247.1 1.4 fusion.22
  250.6 199.1 %reduce-scatter.2.cloned.1.call-done = f32[2,1,16,256]{3,2,1,0:T(8,128)} async-done(((f32[2,1,256,256]{3,2,1,0:T(8,128)}), f32[2,1,16,256]{3,2,1,0:T(8,128)}) %reduce-scatter.2.cloned.1.call-update) | async-done | bytes 32784 | tf_op jit(solution)/shard_map/reduce_scatter | solution.py:133
  449.8 1.4 broadcast_multiply_fusion
  452.3 39.3 %psum.7 = f32[2,16,1]{1,2,0:T(1,128)S(1)} all-reduce(f32[2,16,1]{1,2,0:T(1,128)S(1)} %pad_maximum_fusion.6), channel_id=1, replica_groups=mesh['ka'=16,'ga'=16] {'ga'}, use_global_device_ids=true, to_apply=%region_5.6 | all-reduce | flops 32 | bytes 256 | tf_op jit(solution)/shard_map/psum | solution.py:137
  (243 shorter events, 89.5 us)
Async XLA Ops:
  7.2 104.7 %all-gather.2.cloned.1.call-start = ((), (), s32[]{:S(2)}) async-start(), calls=%async_computation.3 | async-start | bytes 2228224 | tf_op jit(solution)/shard_map/all_gather | solution.py:119
  32.6 54.9 %all-to-all-start = ((bf16[2,16,16,256]{3,2,0,1:T(8,128)(2,1)}), bf16[2,16,16,256]{3,2,0,1:T(8,128)(2,1)S(1)}, u32[]{:S(2)}, u32[]{:S(2)}) async-start(bf16[2,16,16,256]{3,2,0,1:T(8,128)(2,1)} %copy.63), calls=%async_computation | async-start | bytes 524288 | tf_op jit(solution)/shard_map/all_to_all | solution.py:122
  36.2 413.6 %reduce-scatter.2.cloned.1.call-start = ((), (), s32[]{:S(2)}) async-start(), calls=%async_computation.4 | async-start | bytes 557056 | tf_op jit(solution)/shard_map/reduce_scatter | solution.py:133
  41.9 74.0 %copy-start.8 = (bf16[1,256,2,256]{1,3,0,2:T(8,128)(2,1)}, bf16[1,256,2,256]{1,3,0,2:T(8,128)(2,1)S(1)}, u32[]{:S(2)}) copy-start(bf16[1,256,2,256]{1,3,0,2:T(8,128)(2,1)S(1)} %get-tuple-element.444) | copy-start | bytes 786436
  116.9 6.8 %collective-permute-start = (bf16[2,1,256,256]{3,2,1,0:T(8,128)(2,1)S(1)}, bf16[2,1,256,256]{3,2,1,0:T(8,128)(2,1)}, u32[]{:S(2)}, u32[]{:S(2)}) collective-permute-start(bf16[2,1,256,256]{3,2,1,0:T(8,128)(2,1)S(1)} %copy.126), channel_id=1, source_target_pairs={{0,16},{16,32},{32,48},{48,64},{64,80},{80,96},{96,112},{112,128},... | collective-permute-start | bytes 786440 | tf_op jit(solution)/shard_map/while/body/eval_jaxpr/ppermute | solution.py:16
  124.6 6.8 %collective-permute-start = (bf16[2,1,256,256]{3,2,1,0:T(8,128)(2,1)S(1)}, bf16[2,1,256,256]{3,2,1,0:T(8,128)(2,1)}, u32[]{:S(2)}, u32[]{:S(2)}) collective-permute-start(bf16[2,1,256,256]{3,2,1,0:T(8,128)(2,1)S(1)} %copy.126), channel_id=1, source_target_pairs={{0,16},{16,32},{32,48},{48,64},{64,80},{80,96},{96,112},{112,128},... | collective-permute-start | bytes 786440 | tf_op jit(solution)/shard_map/while/body/eval_jaxpr/ppermute | solution.py:16
  132.4 6.8 %collective-permute-start = (bf16[2,1,256,256]{3,2,1,0:T(8,128)(2,1)S(1)}, bf16[2,1,256,256]{3,2,1,0:T(8,128)(2,1)}, u32[]{:S(2)}, u32[]{:S(2)}) collective-permute-start(bf16[2,1,256,256]{3,2,1,0:T(8,128)(2,1)S(1)} %copy.126), channel_id=1, source_target_pairs={{0,16},{16,32},{32,48},{48,64},{64,80},{80,96},{96,112},{112,128},... | collective-permute-start | bytes 786440 | tf_op jit(solution)/shard_map/while/body/eval_jaxpr/ppermute | solution.py:16
  140.1 6.8 %collective-permute-start = (bf16[2,1,256,256]{3,2,1,0:T(8,128)(2,1)S(1)}, bf16[2,1,256,256]{3,2,1,0:T(8,128)(2,1)}, u32[]{:S(2)}, u32[]{:S(2)}) collective-permute-start(bf16[2,1,256,256]{3,2,1,0:T(8,128)(2,1)S(1)} %copy.126), channel_id=1, source_target_pairs={{0,16},{16,32},{32,48},{48,64},{64,80},{80,96},{96,112},{112,128},... | collective-permute-start | bytes 786440 | tf_op jit(solution)/shard_map/while/body/eval_jaxpr/ppermute | solution.py:16
  147.9 6.8 %collective-permute-start = (bf16[2,1,256,256]{3,2,1,0:T(8,128)(2,1)S(1)}, bf16[2,1,256,256]{3,2,1,0:T(8,128)(2,1)}, u32[]{:S(2)}, u32[]{:S(2)}) collective-permute-start(bf16[2,1,256,256]{3,2,1,0:T(8,128)(2,1)S(1)} %copy.126), channel_id=1, source_target_pairs={{0,16},{16,32},{32,48},{48,64},{64,80},{80,96},{96,112},{112,128},... | collective-permute-start | bytes 786440 | tf_op jit(solution)/shard_map/while/body/eval_jaxpr/ppermute | solution.py:16
  155.6 7.4 %collective-permute-start = (bf16[2,1,256,256]{3,2,1,0:T(8,128)(2,1)S(1)}, bf16[2,1,256,256]{3,2,1,0:T(8,128)(2,1)}, u32[]{:S(2)}, u32[]{:S(2)}) collective-permute-start(bf16[2,1,256,256]{3,2,1,0:T(8,128)(2,1)S(1)} %copy.126), channel_id=1, source_target_pairs={{0,16},{16,32},{32,48},{48,64},{64,80},{80,96},{96,112},{112,128},... | collective-permute-start | bytes 786440 | tf_op jit(solution)/shard_map/while/body/eval_jaxpr/ppermute | solution.py:16
  164.0 8.0 %collective-permute-start = (bf16[2,1,256,256]{3,2,1,0:T(8,128)(2,1)S(1)}, bf16[2,1,256,256]{3,2,1,0:T(8,128)(2,1)}, u32[]{:S(2)}, u32[]{:S(2)}) collective-permute-start(bf16[2,1,256,256]{3,2,1,0:T(8,128)(2,1)S(1)} %copy.126), channel_id=1, source_target_pairs={{0,16},{16,32},{32,48},{48,64},{64,80},{80,96},{96,112},{112,128},... | collective-permute-start | bytes 786440 | tf_op jit(solution)/shard_map/while/body/eval_jaxpr/ppermute | solution.py:16
  173.0 8.0 %collective-permute-start = (bf16[2,1,256,256]{3,2,1,0:T(8,128)(2,1)S(1)}, bf16[2,1,256,256]{3,2,1,0:T(8,128)(2,1)}, u32[]{:S(2)}, u32[]{:S(2)}) collective-permute-start(bf16[2,1,256,256]{3,2,1,0:T(8,128)(2,1)S(1)} %copy.126), channel_id=1, source_target_pairs={{0,16},{16,32},{32,48},{48,64},{64,80},{80,96},{96,112},{112,128},... | collective-permute-start | bytes 786440 | tf_op jit(solution)/shard_map/while/body/eval_jaxpr/ppermute | solution.py:16
  181.9 8.0 %collective-permute-start = (bf16[2,1,256,256]{3,2,1,0:T(8,128)(2,1)S(1)}, bf16[2,1,256,256]{3,2,1,0:T(8,128)(2,1)}, u32[]{:S(2)}, u32[]{:S(2)}) collective-permute-start(bf16[2,1,256,256]{3,2,1,0:T(8,128)(2,1)S(1)} %copy.126), channel_id=1, source_target_pairs={{0,16},{16,32},{32,48},{48,64},{64,80},{80,96},{96,112},{112,128},... | collective-permute-start | bytes 786440 | tf_op jit(solution)/shard_map/while/body/eval_jaxpr/ppermute | solution.py:16
  190.9 8.0 %collective-permute-start = (bf16[2,1,256,256]{3,2,1,0:T(8,128)(2,1)S(1)}, bf16[2,1,256,256]{3,2,1,0:T(8,128)(2,1)}, u32[]{:S(2)}, u32[]{:S(2)}) collective-permute-start(bf16[2,1,256,256]{3,2,1,0:T(8,128)(2,1)S(1)} %copy.126), channel_id=1, source_target_pairs={{0,16},{16,32},{32,48},{48,64},{64,80},{80,96},{96,112},{112,128},... | collective-permute-start | bytes 786440 | tf_op jit(solution)/shard_map/while/body/eval_jaxpr/ppermute | solution.py:16
  199.9 8.0 %collective-permute-start = (bf16[2,1,256,256]{3,2,1,0:T(8,128)(2,1)S(1)}, bf16[2,1,256,256]{3,2,1,0:T(8,128)(2,1)}, u32[]{:S(2)}, u32[]{:S(2)}) collective-permute-start(bf16[2,1,256,256]{3,2,1,0:T(8,128)(2,1)S(1)} %copy.126), channel_id=1, source_target_pairs={{0,16},{16,32},{32,48},{48,64},{64,80},{80,96},{96,112},{112,128},... | collective-permute-start | bytes 786440 | tf_op jit(solution)/shard_map/while/body/eval_jaxpr/ppermute | solution.py:16
  208.8 8.0 %collective-permute-start = (bf16[2,1,256,256]{3,2,1,0:T(8,128)(2,1)S(1)}, bf16[2,1,256,256]{3,2,1,0:T(8,128)(2,1)}, u32[]{:S(2)}, u32[]{:S(2)}) collective-permute-start(bf16[2,1,256,256]{3,2,1,0:T(8,128)(2,1)S(1)} %copy.126), channel_id=1, source_target_pairs={{0,16},{16,32},{32,48},{48,64},{64,80},{80,96},{96,112},{112,128},... | collective-permute-start | bytes 786440 | tf_op jit(solution)/shard_map/while/body/eval_jaxpr/ppermute | solution.py:16
  217.8 8.0 %collective-permute-start = (bf16[2,1,256,256]{3,2,1,0:T(8,128)(2,1)S(1)}, bf16[2,1,256,256]{3,2,1,0:T(8,128)(2,1)}, u32[]{:S(2)}, u32[]{:S(2)}) collective-permute-start(bf16[2,1,256,256]{3,2,1,0:T(8,128)(2,1)S(1)} %copy.126), channel_id=1, source_target_pairs={{0,16},{16,32},{32,48},{48,64},{64,80},{80,96},{96,112},{112,128},... | collective-permute-start | bytes 786440 | tf_op jit(solution)/shard_map/while/body/eval_jaxpr/ppermute | solution.py:16
  226.8 8.0 %collective-permute-start = (bf16[2,1,256,256]{3,2,1,0:T(8,128)(2,1)S(1)}, bf16[2,1,256,256]{3,2,1,0:T(8,128)(2,1)}, u32[]{:S(2)}, u32[]{:S(2)}) collective-permute-start(bf16[2,1,256,256]{3,2,1,0:T(8,128)(2,1)S(1)} %copy.126), channel_id=1, source_target_pairs={{0,16},{16,32},{32,48},{48,64},{64,80},{80,96},{96,112},{112,128},... | collective-permute-start | bytes 786440 | tf_op jit(solution)/shard_map/while/body/eval_jaxpr/ppermute | solution.py:16
  235.7 8.0 %collective-permute-start = (bf16[2,1,256,256]{3,2,1,0:T(8,128)(2,1)S(1)}, bf16[2,1,256,256]{3,2,1,0:T(8,128)(2,1)}, u32[]{:S(2)}, u32[]{:S(2)}) collective-permute-start(bf16[2,1,256,256]{3,2,1,0:T(8,128)(2,1)S(1)} %copy.126), channel_id=1, source_target_pairs={{0,16},{16,32},{32,48},{48,64},{64,80},{80,96},{96,112},{112,128},... | collective-permute-start | bytes 786440 | tf_op jit(solution)/shard_map/while/body/eval_jaxpr/ppermute | solution.py:16
  243.7 4.7 copy-start.3
  243.7 4.7 copy-start.5
  243.8 4.7 copy-start.7
  243.8 4.7 copy-start.9
  248.5 2.1 copy-start.1
  (4 other events, 4.0 us)
Sparse Core Ops, SparseCore 0:
  31.1 80.7 all-gather.1
  250.7 199.0 reduce-scatter.1
where the time goes:
time: 501 us; the launch traced here: 499 us
  waiting for transfers between devices  227 us (45%)
  blocking collectives  103 us (21%)
  local copies, waits for them, and re-layouts  56.8 us (11%)
  loops' own time  29.7 us (6%)
  starting transfers between devices  25.6 us (5%)
  matrix products  21.5 us (4%)
  other arithmetic  18.2 us (4%)
  between operations  16.4 us (3%)
    reduce_scatter x1, waiting for transfers between devices, per_device(): lax.psum_scatter(total, 'ga', scatter_dimension=2, tiled=True)  199 us
    all_gather x1, blocking collectives, per_device(): targets = lax.all_gather(orbital_block[:, :NI], 'ga', axis=2, tiled=True)  42.9 us
    psum x1, blocking collectives, per_device(): summed = lax.psum(jnp.stack([intersection_re, intersection_im]), 'ga')  39.3 us
    another operation x1, loops' own time, cycle_total(): total, visitor = lax.fori_loop(0, cycle_length - 1, turn, (start, held))  29.7 us
    all_gather x1, waiting for transfers between devices, per_device(): lax.all_gather(kernel_block.astype(jnp.bfloat16), 'ga', axis=1, tiled=True)  23.6 us
    ppermute x15, starting transfers between devices, passed_along(): lax.ppermute(shard, axis, [(i, (i + by) % peers) for i in range(peers)])  22 us
    all_to_all x1, blocking collectives, per_device(): lax.all_to_all(outgoing.astype(jnp.bfloat16), 'ga', split_axis=1, concat_...  21.1 us
    dynamic_slice x16, local copies, waits for them, and re-layouts, contrib(): q_index[my_kpoint, partner_k]  20.9 us
  transfers between devices with their start and end apart: 18, of which 7 were waited for; matrix products, arithmetic and copies ran while one was open for 13% of the time, Pallas kernels for 0%

commit v1 on v0

v1 whole, which is shorter than its diff:
```python
import functools
import math

import jax
import jax.numpy as jnp
import numpy as np
from jax import lax
from jax.experimental import pallas as pl
from jax.experimental.pallas import tpu as pltpu
from jax.sharding import PartitionSpec as P

N = 256
GA = 16
ROWS = 16
MESH = pl.DeviceIdType.MESH
bf16, f32, i32 = jnp.bfloat16, jnp.float32, jnp.int32

SPAN, SLOT, PLANE, TARGET, TOTAL, DOT = (16 * i for i in range(6))
SPAN_Y, SPAN_X, SPAN_C, TARGET_C, SUM_C, RING = 96, 97, 100, 101, 102, 103
SEMAPHORES = 112


def dft_blocks():
    ramp = np.arange(N)
    angles = (ramp[:, None] * ramp[None, :] % N).astype(np.float32) * np.float32(2.0 * math.pi / N)
    cosine, sine = np.cos(angles).astype(np.float32), np.sin(angles).astype(np.float32)
    first = np.block([[cosine, -sine], [sine, cosine]])
    second = np.block([[cosine, sine], [-sine, cosine]])
    return np.stack([first, second]).astype(jnp.bfloat16)


def dot(left, right):
    return jnp.dot(left, right, preferred_element_type=f32)


def density(target, partner):
    target_re, target_im = target[0].astype(f32), target[1].astype(f32)
    partner_re, partner_im = partner[0].astype(f32), partner[1].astype(f32)
    re = target_re * partner_re + target_im * partner_im
    im = target_im * partner_re - target_re * partner_im
    return jnp.concatenate([re.astype(bf16), im.astype(bf16)], axis=1)


def kernel(
    orbitals, spans, owner, q_index, tables, image, intersections,
    dft, own, slots, targets, span_block, span_out, slot_rows, slot_out, weights, kernels,
    half, weighted, returned, acc, to_core, from_core, to_ga, from_ga, dots, dot_out,
    send, recv, local,
):
    ka, ga = lax.axis_index("ka"), lax.axis_index("ga")
    x, y, c = ka // 4, (ka // 2) % 2, ka % 2
    along_x = [(((x + i) % 4) * 4 + y * 2 + c, ga) for i in range(4)]
    other_y = (x * 4 + (1 - y) * 2 + c, ga)
    other_c = (x * 4 + y * 2 + (1 - c), ga)

    def ga_peer(i):
        return (ka, lax.rem(ga + i, GA))

    barrier = pltpu.get_barrier_semaphore()
    for i in range(1, GA):
        pl.semaphore_signal(barrier, inc=1, device_id=ga_peer(i), device_id_type=MESH)
    for peer in along_x[1:] + [other_y, other_c]:
        pl.semaphore_signal(barrier, inc=1, device_id=peer, device_id_type=MESH)

    def rows_of(block):
        return pl.ds(pl.multiple_of(block * ROWS, ROWS), ROWS)

    def remote(src, dst, number, peer):
        return pltpu.make_async_remote_copy(src, dst, send.at[number], recv.at[number], peer, MESH)

    copies = [
        pltpu.make_async_copy(tables, dft, local.at[0]),
        pltpu.make_async_copy(orbitals.at[0], own, local.at[1]),
        pltpu.make_async_copy(orbitals.at[0, :, ga], slots.at[0, :, rows_of(ga)], local.at[2]),
        pltpu.make_async_copy(orbitals.at[0, :, 0], targets.at[0, :, rows_of(ga)], local.at[3]),
    ]
    for copy in copies:
        copy.start()

    span_out[...] = spans[ka].astype(bf16)
    span_block[ga] = span_out[...]
    owners = jnp.broadcast_to(owner[ka], (ROWS, 128))
    place = lax.broadcasted_iota(i32, (ROWS, 128), 0)
    arrival = jnp.zeros((ROWS, 128), i32)
    for earlier in range(ROWS - 1):
        same = (owners == owners[earlier : earlier + 1]) & (place > earlier)
        arrival = arrival + same.astype(i32)
    lane = lax.broadcasted_iota(i32, (ROWS, 128), 1)
    mine = lane == lax.rem(ga, 8) * ROWS + place
    slot = jnp.where(mine, (owners * 2 + arrival).astype(f32), 0.0)
    slot_out[...] = jnp.sum(slot, axis=0, keepdims=True)
    slot_rows[ga] = slot_out[...]

    pl.semaphore_wait(barrier, 20)

    def send_span(i):
        return remote(span_out, span_block.at[ga], SPAN + i, ga_peer(i))

    def send_slot(i):
        return remote(slot_out, slot_rows.at[ga], SLOT + i, ga_peer(i))

    def send_plane(i):
        peer = ga_peer(i)
        return remote(orbitals.at[0, :, peer[1]], slots.at[0, :, rows_of(ga)], PLANE + i, peer)

    def send_target(i):
        return remote(orbitals.at[0, :, 0], targets.at[0, :, rows_of(ga)], TARGET + i, ga_peer(i))

    def over_ga(*sends):
        @pl.loop(1, GA)
        def _(i):
            for one in sends:
                one(i).start()

    def arrived(one):
        @pl.loop(1, GA)
        def _(i):
            one(i).wait_recv()

    over_ga(send_span, send_slot)
    over_ga(send_plane)
    over_ga(send_target)

    arrived(send_span)
    arrived(send_slot)
    block = span_block[...].reshape(N, 128).astype(f32)
    weights[x, y, c, 0:128] = jnp.transpose(block).astype(bf16)
    low = jnp.sum(slot_rows[0:8], axis=0)
    high = jnp.sum(slot_rows[8:16], axis=0)
    slot_line = jnp.concatenate([low, high], axis=1)
    weights[x, y, c, 128:144] = jnp.broadcast_to(slot_line, (16, N)).astype(bf16)

    span_y = remote(weights.at[x, y, c], weights.at[x, y, c], SPAN_Y, other_y)
    span_y.start()
    span_y.wait_recv()
    span_x = [
        remote(weights.at[x, :, c], weights.at[x, :, c], SPAN_X + n, along_x[i])
        for n, i in enumerate((1, 3, 2))
    ]
    for copy in span_x:
        copy.start()

    for copy in copies:
        copy.wait()
    arrived(send_plane)

    lower, upper = pl.ds(0, 128), pl.ds(128, 128)

    def ring(number, source, rows, sink, peer):
        if rows is None:
            return remote(slots.at[source], slots.at[sink], RING + number, peer)
        return remote(
            slots.at[source, :, rows], slots.at[sink, :, rows], RING + number, peer
        )

    back, ahead = along_x[3], along_x[1]
    own_back, own_ahead = ring(0, 0, None, 1, back), ring(1, 0, None, 3, ahead)
    own_y = ring(2, 0, None, 4, other_y)
    relay_back, relay_ahead = ring(3, 1, lower, 2, back), ring(4, 3, upper, 2, ahead)
    y_back, y_ahead = ring(5, 4, None, 5, back), ring(6, 4, None, 7, ahead)
    y_relay_back, y_relay_ahead = ring(7, 5, lower, 6, back), ring(8, 7, upper, 6, ahead)
    rings = [
        own_back, own_ahead, own_y, relay_back, relay_ahead,
        y_back, y_ahead, y_relay_back, y_relay_ahead,
    ]
    own_back.start()
    own_ahead.start()
    own_y.start()

    arrived(send_target)
    target_c = remote(targets.at[0], targets.at[1], TARGET_C, other_c)
    target_c.start()

    for copy in span_x:
        copy.wait_recv()
    span_c = remote(weights.at[:, :, c], weights.at[:, :, c], SPAN_C, other_c)
    span_c.start()
    target_c.wait_recv()
    span_c.wait_recv()

    k_of_target = (ka, x * 4 + y * 2 + (1 - c))

    def expand(slot_number):
        dy, dx = slot_number // 4, slot_number % 4
        partner_k = ((x + dx) % 4) * 4 + (y ^ 1 if dy else y) * 2 + c
        group = lax.broadcasted_iota(i32, (N, N), 1) // ROWS
        g2 = lax.broadcasted_iota(i32, (N, N), 0)
        wanted = ((g2 // ROWS) * 2 + (g2 % ROWS - group) * 64).astype(f32)
        for t in range(2):
            q = q_index[k_of_target[t], partner_k]
            table = weights[lax.div(q, 4), lax.rem(lax.div(q, 2), 2), lax.rem(q, 2)]
            line = table[128:129].astype(f32)
            for arrival_number in range(2):
                hot = (line == wanted + float(arrival_number)).astype(f32).astype(bf16)
                part = lax.dot_general(
                    table[0:128], hot, (((1,), (1,)), ((), ())), preferred_element_type=f32
                )
                kernels[slot_number * 2 + t, arrival_number * 128 : arrival_number * 128 + 128] = (
                    part.astype(bf16)
                )

    def pairs(slot_numbers, first):
        work = [(s, t) for s in slot_numbers for t in range(2)]
        for n, (s, t) in enumerate(work):
            h = dot(density(targets.at[t], slots.at[s]), dft[0]).astype(bf16)
            half[0:N, n * N : n * N + N] = h[:, 0:N]
            half[N : 2 * N, n * N : n * N + N] = h[:, N : 2 * N]
        for n, (s, t) in enumerate(work):
            spectrum = dot(dft[1], half[:, n * N : n * N + N])
            factor = kernels[s * 2 + t].astype(f32)
            weighted[0:N, n * N : n * N + N] = (spectrum[0:N] * factor).astype(bf16)
            weighted[N : 2 * N, n * N : n * N + N] = (spectrum[N : 2 * N] * factor).astype(bf16)
        for n in range(len(work)):
            r = dot(dft[0], weighted[:, n * N : n * N + N]).astype(bf16)
            returned[n * N : n * N + N, 0:N] = r[0:N]
            returned[n * N : n * N + N, N : 2 * N] = r[N : 2 * N]
        for n, (s, t) in enumerate(work):
            potential = dot(returned[n * N : n * N + N, :], dft[1])
            partner_re, partner_im = slots[s, 0].astype(f32), slots[s, 1].astype(f32)
            v_re, v_im = potential[:, 0:N], potential[:, N : 2 * N]
            add_re = v_re * partner_re - v_im * partner_im
            add_im = v_re * partner_im + v_im * partner_re
            if first:
                acc[t, 0] = add_re
                acc[t, 1] = add_im
            else:
                acc[t, 0] += add_re
                acc[t, 1] += add_im

    expand(0)
    pairs((0,), True)
    for s in (1, 3, 4, 2, 5, 7, 6):
        expand(s)
    own_back.wait_recv()
    relay_back.start()
    own_ahead.wait_recv()
    relay_ahead.start()
    own_y.wait_recv()
    y_back.start()
    y_ahead.start()
    pairs((1, 3), False)
    relay_back.wait_recv()
    relay_ahead.wait_recv()
    pairs((4, 2), False)
    y_back.wait_recv()
    y_relay_back.start()
    y_ahead.wait_recv()
    y_relay_ahead.start()
    pairs((5, 7), False)
    y_relay_back.wait_recv()
    y_relay_ahead.wait_recv()
    pairs((6,), False)

    to_core[...] = acc[1].astype(bf16)
    sum_c = remote(to_core, from_core, SUM_C, other_c)
    sum_c.start()
    sum_c.wait_recv()
    to_ga[...] = (acc[0] + from_core[...].astype(f32)).astype(bf16)

    def send_total(i):
        peer = ga_peer(i)
        return remote(to_ga.at[:, rows_of(peer[1])], from_ga.at[ga], TOTAL + i, peer)

    over_ga(send_total)
    from_ga[ga] = to_ga[:, rows_of(ga)]
    arrived(send_total)
    total = jnp.sum(from_ga[...].astype(f32), axis=0) * (-1.0 / (16 * N * N))
    image[0, 0, 0] = total[0]
    image[0, 1, 0] = total[1]

    own_re, own_im = own[0].astype(f32), own[1].astype(f32)
    re = jnp.sum(own_re * total[0][None] + own_im * total[1][None], axis=1)
    im = jnp.sum(own_re * total[1][None] - own_im * total[0][None], axis=1)
    re = jnp.broadcast_to(jnp.sum(re, axis=1, keepdims=True), (16, 128))
    im = jnp.broadcast_to(jnp.sum(im, axis=1, keepdims=True), (16, 128))
    both = jnp.where(lane == place, re, 0.0) + jnp.where(lane == place + 16, im, 0.0)
    dot_out[...] = jnp.sum(both, axis=0, keepdims=True)

    def send_dots(i):
        return remote(dot_out, dots.at[ga], DOT + i, ga_peer(i))

    over_ga(send_dots)
    dots[ga] = dot_out[...]
    arrived(send_dots)
    line = jnp.broadcast_to(jnp.sum(dots[...], axis=0) * (1.0 / N), (16, 128))
    intersections[0, 0] = jnp.sum(jnp.where(lane == place, line, 0.0), axis=1, keepdims=True)
    intersections[0, 1] = jnp.sum(jnp.where(lane == place + 16, line, 0.0), axis=1, keepdims=True)

    for one in (send_span, send_slot, send_plane, send_target, send_total, send_dots):

        @pl.loop(1, GA)
        def _(i):
            one(i).wait_send()

    for copy in [span_y, *span_x, span_c, target_c, sum_c, *rings]:
        copy.wait_send()


def per_device(orbitals, kernel_spans, span_owner, q_index):
    vmem, anywhere = pl.BlockSpec(memory_space=pltpu.VMEM), pl.BlockSpec(memory_space=pl.ANY)
    plane = (2, N, N)
    return tuple(
        pl.pallas_call(
            kernel,
            out_shape=(
                jax.ShapeDtypeStruct((1, 2, 1, ROWS, N), f32),
                jax.ShapeDtypeStruct((1, 2, 16, 1), f32),
            ),
            in_specs=[anywhere, vmem, vmem, pl.BlockSpec(memory_space=pltpu.SMEM), anywhere],
            out_specs=(vmem, vmem),
            scratch_shapes=[
                pltpu.VMEM((2, 2 * N, 2 * N), bf16),
                pltpu.VMEM((2, 16, ROWS, N), bf16),
                pltpu.VMEM((8, *plane), bf16),
                pltpu.VMEM((2, *plane), bf16),
                pltpu.VMEM((GA, ROWS, 128), bf16),
                pltpu.VMEM((ROWS, 128), bf16),
                pltpu.VMEM((GA, 1, 128), f32),
                pltpu.VMEM((1, 128), f32),
                pltpu.VMEM((4, 2, 2, 144, N), bf16),
                pltpu.VMEM((16, N, N), bf16),
                pltpu.VMEM((2 * N, 4 * N), bf16),
                pltpu.VMEM((2 * N, 4 * N), bf16),
                pltpu.VMEM((4 * N, 2 * N), bf16),
                pltpu.VMEM((2, *plane), f32),
                pltpu.VMEM(plane, bf16),
                pltpu.VMEM(plane, bf16),
                pltpu.VMEM(plane, bf16),
                pltpu.VMEM((GA, 2, ROWS, N), bf16),
                pltpu.VMEM((GA, 1, 128), f32),
                pltpu.VMEM((1, 128), f32),
                pltpu.SemaphoreType.DMA((SEMAPHORES,)),
                pltpu.SemaphoreType.DMA((SEMAPHORES,)),
                pltpu.SemaphoreType.DMA((4,)),
            ],
            compiler_params=pltpu.CompilerParams(
                collective_id=0, has_side_effects=True, vmem_limit_bytes=40 * 2**20
            ),
        )(orbitals, kernel_spans, span_owner, q_index, jnp.asarray(dft_blocks()))
    )


def solution(mesh):
    in_specs = (P("ka", None, None, "ga", None), P(None, "ga", None), P(None, "ga", None), P())
    out_specs = (P("ka", None, None, "ga", None), P("ka", None, None, None))
    return jax.shard_map(
        per_device, mesh=mesh, in_specs=in_specs, out_specs=out_specs, check_vma=False
    )
```

time: 501 us -> 76.2 us (0.15)
  the two profiles are of different devices: /device:TPU:6 before, /device:TPU:1 now
where the time goes in v1:
time: 76.2 us; the launch traced here: 76.1 us
  Pallas kernels  71.1 us (93%)
  local copies, waits for them, and re-layouts  4.35 us (6%)
    pallas_call x1, Pallas kernels, per_device(): pl.pallas_call(kernel, out_shape=(jax.ShapeDtypeStruct((1, 2, 1, ROWS, N)...  71.1 us
    unnamed x10, local copies, waits for them, and re-layouts  3.71 us

profile of v1, /device:TPU:1, one launch (start us, length us, event | category | flops | bytes accessed | tf_op | source)
XLA Modules:
  0.0 76.1 jit_solution(2231228001921117457)
XLA Ops:
  0.6 0.0 copy-start.3
  0.6 0.0 copy-start.2
  0.7 0.9 %copy.7.owner = s32[16,16,1]{2,1,0:T(8,128)S(1)} copy(s32[16,16,1]{1,2,0:T(1,128)} %param.7) | data formatting | bytes 2048 | tf_op args[2]
  1.5 0.0 copy-done.3
  1.6 0.0 copy-done.2
  1.6 0.0 copy-start
  1.6 1.2 %copy-done = bf16[2,512,512]{2,1,0:T(8,128)(2,1)S(1)} copy-done((bf16[2,512,512]{2,1,0:T(8,128)(2,1)S(1)}, bf16[2,512,512]{2,1,0:T(8,128)(2,1)}, u32[]{:S(2)}) %copy-start) | copy-done | bytes 1048600
  2.8 0.0 copy-start.1
  2.8 0.9 %copy-done.1 = bf16[1,2,16,16,256]{4,3,2,1,0:T(8,128)(2,1)S(1)} copy-done((bf16[1,2,16,16,256]{4,3,2,1,0:T(8,128)(2,1)S(1)}, bf16[1,2,16,16,256]{4,3,2,1,0:T(8,128)(2,1)}, u32[]{:S(2)}) %copy-start.1) | copy-done | bytes 262168
  3.7 71.1 %shard_map.68 = (f32[1,2,1,16,256]{4,3,2,1,0:T(8,128)S(1)}, f32[1,2,16,1]{3,2,1,0:T(8,128)S(1)}) custom-call(bf16[1,2,16,16,256]{4,3,2,1,0:T(8,128)(2,1)S(1)} %copy-done.1, f32[16,16,128]{2,1,0:T(8,128)S(1)} %copy-done.2, s32[16,16,1]{2,1,0:T(8,128)S(1)} %copy.7.owner, s32[16,16]{1,0:T(8,128)S(1)} %copy-done.3, bf16[2,512,512]{2,1,0:T(8,128)(2,1)S(1)} %copy-done), custom_call_target="tpu_custom_call" | custom-call | tf_op jit(solution)/shard_map/pallas_call | solution.py:303
  74.8 0.6 copy.8
  75.5 0.6 copy.10
Async XLA Ops:
  0.6 0.9 %copy-start.3 = (s32[16,16]{1,0:T(8,128)S(1)}, s32[16,16]{1,0:T(8,128)}, u32[]{:S(2)}) copy-start(s32[16,16]{1,0:T(8,128)} %q_index.1) | copy-start | bytes 3076
  0.6 0.9 %copy-start.2 = (f32[16,16,128]{2,1,0:T(8,128)S(1)}, f32[16,16,128]{2,1,0:T(8,128)}, u32[]{:S(2)}) copy-start(f32[16,16,128]{2,1,0:T(8,128)} %spans.1) | copy-start | bytes 393220
  1.6 1.2 %copy-start = (bf16[2,512,512]{2,1,0:T(8,128)(2,1)S(1)}, bf16[2,512,512]{2,1,0:T(8,128)(2,1)}, u32[]{:S(2)}) copy-start(bf16[2,512,512]{2,1,0:T(8,128)(2,1)} %constant.2.clone.tables) | copy-start | bytes 3145732
  2.8 0.9 %copy-start.1 = (bf16[1,2,16,16,256]{4,3,2,1,0:T(8,128)(2,1)S(1)}, bf16[1,2,16,16,256]{4,3,2,1,0:T(8,128)(2,1)}, u32[]{:S(2)}) copy-start(bf16[1,2,16,16,256]{4,3,2,1,0:T(8,128)(2,1)} %orbitals.1) | copy-start | bytes 786436

commit v2 on v1

--- a/solution.py
+++ b/solution.py
@@ -17,7 +17,7 @@
 
 SPAN, SLOT, PLANE, TARGET, TOTAL, DOT = (16 * i for i in range(6))
 SPAN_Y, SPAN_X, SPAN_C, TARGET_C, SUM_C, RING = 96, 97, 100, 101, 102, 103
-SEMAPHORES = 112
+SEMAPHORES = 120
 
 
 def dft_blocks():
@@ -43,7 +43,7 @@
 
 def kernel(
     orbitals, spans, owner, q_index, tables, image, intersections,
-    dft, own, slots, targets, span_block, span_out, slot_rows, slot_out, weights, kernels,
+    dft, own, slots, targets, span_wide, span_block, span_out, slot_rows, slot_out, weights, kernels,
     half, weighted, returned, acc, to_core, from_core, to_ga, from_ga, dots, dot_out,
     send, recv, local,
 ):
@@ -74,22 +74,27 @@
         pltpu.make_async_copy(orbitals.at[0, :, ga], slots.at[0, :, rows_of(ga)], local.at[2]),
         pltpu.make_async_copy(orbitals.at[0, :, 0], targets.at[0, :, rows_of(ga)], local.at[3]),
     ]
+    wide = pltpu.make_async_copy(spans.at[ka], span_wide, local.at[4])
+    wide.start()
     for copy in copies:
         copy.start()
 
-    span_out[...] = spans[ka].astype(bf16)
-    span_block[ga] = span_out[...]
-    owners = jnp.broadcast_to(owner[ka], (ROWS, 128))
     place = lax.broadcasted_iota(i32, (ROWS, 128), 0)
-    arrival = jnp.zeros((ROWS, 128), i32)
+    lane = lax.broadcasted_iota(i32, (ROWS, 128), 1)
+    line = jnp.broadcast_to(owner[ka].astype(f32), (ROWS, ROWS))
+    line = jnp.where(lane[:, 0:ROWS] == place[:, 0:ROWS], line, 0.0)
+    owners = jnp.broadcast_to(jnp.sum(line, axis=1, keepdims=True), (ROWS, 128))
+    arrival = jnp.zeros((ROWS, 128), f32)
     for earlier in range(ROWS - 1):
         same = (owners == owners[earlier : earlier + 1]) & (place > earlier)
-        arrival = arrival + same.astype(i32)
-    lane = lax.broadcasted_iota(i32, (ROWS, 128), 1)
+        arrival = arrival + jnp.where(same, 1.0, 0.0)
     mine = lane == lax.rem(ga, 8) * ROWS + place
-    slot = jnp.where(mine, (owners * 2 + arrival).astype(f32), 0.0)
+    slot = jnp.where(mine, owners * 2.0 + arrival, 0.0)
     slot_out[...] = jnp.sum(slot, axis=0, keepdims=True)
     slot_rows[ga] = slot_out[...]
+    wide.wait()
+    span_out[...] = span_wide[...].astype(bf16)
+    span_block[ga] = span_out[...]
 
     pl.semaphore_wait(barrier, 20)
 
@@ -119,7 +124,6 @@
 
     over_ga(send_span, send_slot)
     over_ga(send_plane)
-    over_ga(send_target)
 
     arrived(send_span)
     arrived(send_slot)
@@ -132,6 +136,29 @@
 
     span_y = remote(weights.at[x, y, c], weights.at[x, y, c], SPAN_Y, other_y)
     span_y.start()
+    for copy in copies:
+        copy.wait()
+    arrived(send_plane)
+
+    lower, upper = pl.ds(0, 128), pl.ds(128, 128)
+    quarters = pl.ds(0, 64), pl.ds(64, 64)
+    back, ahead = along_x[3], along_x[1]
+    rings = []
+
+    def ring(source, rows, sink, peer):
+        rings.append(
+            remote(
+                slots.at[source, :, rows], slots.at[sink, :, rows], RING + len(rings), peer
+            )
+        )
+        rings[-1].start()
+        return rings[-1]
+
+    up1, up3, low4 = ring(0, upper, 1, back), ring(0, upper, 3, ahead), ring(0, lower, 4, other_y)
+    low1, low3, up4 = ring(0, lower, 1, back), ring(0, lower, 3, ahead), ring(0, upper, 4, other_y)
+
+    over_ga(send_target)
+
     span_y.wait_recv()
     span_x = [
         remote(weights.at[x, :, c], weights.at[x, :, c], SPAN_X + n, along_x[i])
@@ -140,42 +167,31 @@
     for copy in span_x:
         copy.start()
 
-    for copy in copies:
-        copy.wait()
-    arrived(send_plane)
-
-    lower, upper = pl.ds(0, 128), pl.ds(128, 128)
-
-    def ring(number, source, rows, sink, peer):
-        if rows is None:
-            return remote(slots.at[source], slots.at[sink], RING + number, peer)
-        return remote(
-            slots.at[source, :, rows], slots.at[sink, :, rows], RING + number, peer
-        )
-
-    back, ahead = along_x[3], along_x[1]
-    own_back, own_ahead = ring(0, 0, None, 1, back), ring(1, 0, None, 3, ahead)
-    own_y = ring(2, 0, None, 4, other_y)
-    relay_back, relay_ahead = ring(3, 1, lower, 2, back), ring(4, 3, upper, 2, ahead)
-    y_back, y_ahead = ring(5, 4, None, 5, back), ring(6, 4, None, 7, ahead)
-    y_relay_back, y_relay_ahead = ring(7, 5, lower, 6, back), ring(8, 7, upper, 6, ahead)
-    rings = [
-        own_back, own_ahead, own_y, relay_back, relay_ahead,
-        y_back, y_ahead, y_relay_back, y_relay_ahead,
-    ]
-    own_back.start()
-    own_ahead.start()
-    own_y.start()
+    up1.wait_recv()
+    up5 = ring(1, upper, 5, other_y)
+    low4.wait_recv()
+    low5, low7 = ring(4, lower, 5, back), ring(4, lower, 7, ahead)
+    up3.wait_recv()
+    up7 = ring(3, upper, 7, other_y)
+    up2 = ring(1, upper, 2, back)
+    low3.wait_recv()
+    low2 = ring(3, lower, 2, ahead)
 
     arrived(send_target)
     target_c = remote(targets.at[0], targets.at[1], TARGET_C, other_c)
     target_c.start()
-
     for copy in span_x:
         copy.wait_recv()
     span_c = remote(weights.at[:, :, c], weights.at[:, :, c], SPAN_C, other_c)
     span_c.start()
-    target_c.wait_recv()
+
+    low5.wait_recv()
+    first6 = ring(5, quarters[0], 6, back)
+    low7.wait_recv()
+    second6 = ring(7, quarters[1], 6, ahead)
+    up5.wait_recv()
+    up6 = ring(5, upper, 6, back)
+
     span_c.wait_recv()
 
     k_of_target = (ka, x * 4 + y * 2 + (1 - c))
@@ -220,36 +236,28 @@
             v_re, v_im = potential[:, 0:N], potential[:, N : 2 * N]
             add_re = v_re * partner_re - v_im * partner_im
             add_im = v_re * partner_im + v_im * partner_re
-            if first:
+            if first and n < 2:
                 acc[t, 0] = add_re
                 acc[t, 1] = add_im
             else:
                 acc[t, 0] += add_re
                 acc[t, 1] += add_im
 
-    expand(0)
-    pairs((0,), True)
-    for s in (1, 3, 4, 2, 5, 7, 6):
+    for s in range(8):
         expand(s)
-    own_back.wait_recv()
-    relay_back.start()
-    own_ahead.wait_recv()
-    relay_ahead.start()
-    own_y.wait_recv()
-    y_back.start()
-    y_ahead.start()
-    pairs((1, 3), False)
-    relay_back.wait_recv()
-    relay_ahead.wait_recv()
-    pairs((4, 2), False)
-    y_back.wait_recv()
-    y_relay_back.start()
-    y_ahead.wait_recv()
-    y_relay_ahead.start()
-    pairs((5, 7), False)
-    y_relay_back.wait_recv()
-    y_relay_ahead.wait_recv()
-    pairs((6,), False)
+    target_c.wait_recv()
+    low1.wait_recv()
+    pairs((0, 1), True)
+    up4.wait_recv()
+    pairs((3, 4), False)
+    up2.wait_recv()
+    low2.wait_recv()
+    pairs((2, 5), False)
+    up7.wait_recv()
+    first6.wait_recv()
+    second6.wait_recv()
+    up6.wait_recv()
+    pairs((7, 6), False)
 
     to_core[...] = acc[1].astype(bf16)
     sum_c = remote(to_core, from_core, SUM_C, other_c)
@@ -282,9 +290,9 @@
     over_ga(send_dots)
     dots[ga] = dot_out[...]
     arrived(send_dots)
-    line = jnp.broadcast_to(jnp.sum(dots[...], axis=0) * (1.0 / N), (16, 128))
-    intersections[0, 0] = jnp.sum(jnp.where(lane == place, line, 0.0), axis=1, keepdims=True)
-    intersections[0, 1] = jnp.sum(jnp.where(lane == place + 16, line, 0.0), axis=1, keepdims=True)
+    line = jnp.sum(dots[...], axis=0) * (1.0 / N)
+    intersections[0, 0] = line[:, 0:16]
+    intersections[0, 1] = line[:, 16:32]
 
     for one in (send_span, send_slot, send_plane, send_target, send_total, send_dots):
 
@@ -299,45 +307,45 @@
 def per_device(orbitals, kernel_spans, span_owner, q_index):
     vmem, anywhere = pl.BlockSpec(memory_space=pltpu.VMEM), pl.BlockSpec(memory_space=pl.ANY)
     plane = (2, N, N)
-    return tuple(
-        pl.pallas_call(
-            kernel,
-            out_shape=(
-                jax.ShapeDtypeStruct((1, 2, 1, ROWS, N), f32),
-                jax.ShapeDtypeStruct((1, 2, 16, 1), f32),
-            ),
-            in_specs=[anywhere, vmem, vmem, pl.BlockSpec(memory_space=pltpu.SMEM), anywhere],
-            out_specs=(vmem, vmem),
-            scratch_shapes=[
-                pltpu.VMEM((2, 2 * N, 2 * N), bf16),
-                pltpu.VMEM((2, 16, ROWS, N), bf16),
-                pltpu.VMEM((8, *plane), bf16),
-                pltpu.VMEM((2, *plane), bf16),
-                pltpu.VMEM((GA, ROWS, 128), bf16),
-                pltpu.VMEM((ROWS, 128), bf16),
-                pltpu.VMEM((GA, 1, 128), f32),
-                pltpu.VMEM((1, 128), f32),
-                pltpu.VMEM((4, 2, 2, 144, N), bf16),
-                pltpu.VMEM((16, N, N), bf16),
-                pltpu.VMEM((2 * N, 4 * N), bf16),
-                pltpu.VMEM((2 * N, 4 * N), bf16),
-                pltpu.VMEM((4 * N, 2 * N), bf16),
-                pltpu.VMEM((2, *plane), f32),
-                pltpu.VMEM(plane, bf16),
-                pltpu.VMEM(plane, bf16),
-                pltpu.VMEM(plane, bf16),
-                pltpu.VMEM((GA, 2, ROWS, N), bf16),
-                pltpu.VMEM((GA, 1, 128), f32),
-                pltpu.VMEM((1, 128), f32),
-                pltpu.SemaphoreType.DMA((SEMAPHORES,)),
-                pltpu.SemaphoreType.DMA((SEMAPHORES,)),
-                pltpu.SemaphoreType.DMA((4,)),
-            ],
-            compiler_params=pltpu.CompilerParams(
-                collective_id=0, has_side_effects=True, vmem_limit_bytes=40 * 2**20
-            ),
-        )(orbitals, kernel_spans, span_owner, q_index, jnp.asarray(dft_blocks()))
-    )
+    image, intersections = pl.pallas_call(
+        kernel,
+        out_shape=(
+            jax.ShapeDtypeStruct((1, 2, 1, ROWS, N), f32),
+            jax.ShapeDtypeStruct((1, 2, 1, 16), f32),
+        ),
+        in_specs=[anywhere, anywhere, vmem, pl.BlockSpec(memory_space=pltpu.SMEM), anywhere],
+        out_specs=(vmem, vmem),
+        scratch_shapes=[
+            pltpu.VMEM((2, 2 * N, 2 * N), bf16),
+            pltpu.VMEM((2, 16, ROWS, N), bf16),
+            pltpu.VMEM((8, *plane), bf16),
+            pltpu.VMEM((2, *plane), bf16),
+            pltpu.VMEM((ROWS, 128), f32),
+            pltpu.VMEM((GA, ROWS, 128), bf16),
+            pltpu.VMEM((ROWS, 128), bf16),
+            pltpu.VMEM((GA, 1, 128), f32),
+            pltpu.VMEM((1, 128), f32),
+            pltpu.VMEM((4, 2, 2, 144, N), bf16),
+            pltpu.VMEM((16, N, N), bf16),
+            pltpu.VMEM((2 * N, 4 * N), bf16),
+            pltpu.VMEM((2 * N, 4 * N), bf16),
+            pltpu.VMEM((4 * N, 2 * N), bf16),
+            pltpu.VMEM((2, *plane), f32),
+            pltpu.VMEM(plane, bf16),
+            pltpu.VMEM(plane, bf16),
+            pltpu.VMEM(plane, bf16),
+            pltpu.VMEM((GA, 2, ROWS, N), bf16),
+            pltpu.VMEM((GA, 1, 128), f32),
+            pltpu.VMEM((1, 128), f32),
+            pltpu.SemaphoreType.DMA((SEMAPHORES,)),
+            pltpu.SemaphoreType.DMA((SEMAPHORES,)),
+            pltpu.SemaphoreType.DMA((5,)),
+        ],
+        compiler_params=pltpu.CompilerParams(
+            collective_id=0, has_side_effects=True, vmem_limit_bytes=60 * 2**20
+        ),
+    )(orbitals, kernel_spans, span_owner.reshape(16, 1, ROWS), q_index, jnp.asarray(dft_blocks()))
+    return image, intersections.reshape(1, 2, 16, 1)
 
 
 def solution(mesh):

time: 76.2 us -> 74 us (0.971)
  local copies, waits for them, and re-layouts: 4.35 us -> 1.94 us
    unnamed x10 -> x4, local copies, waits for them, and re-layouts: 3.71 us -> 1.94 us
where the time goes in v2:
time: 74 us; the launch traced here: 73.7 us
  Pallas kernels  71.1 us (96%)
  local copies, waits for them, and re-layouts  1.94 us (3%)
    pallas_call x1, Pallas kernels, per_device(): pl.pallas_call(kernel, out_shape=(jax.ShapeDtypeStruct((1, 2, 1, ROWS, N)...  71.1 us
    unnamed x4, local copies, waits for them, and re-layouts  1.94 us

profile of v2, /device:TPU:1, one launch (start us, length us, event | category | flops | bytes accessed | tf_op | source)
XLA Modules:
  0.0 73.7 jit_solution(14642692655322221541)
XLA Ops:
  0.6 71.1 %shard_map.68 = (f32[1,2,1,16,256]{4,3,2,1,0:T(8,128)}, f32[1,2,1,16]{3,2,1,0:T(1,128)}) custom-call(bf16[1,2,16,16,256]{4,3,2,1,0:T(8,128)(2,1)} %orbitals.1, f32[16,16,128]{2,1,0:T(8,128)} %spans.1, s32[16,1,16]{2,1,0:T(1,128)} %bitcast.4, s32[16,16]{1,0:T(8,128)} %q_index.1, bf16[2,512,512]{2,1,0:T(8,128)(2,1)} %constant.2.clone.tables), custom_call_target="tpu_custom_call" | custom-call | tf_op jit(solution)/shard_map/pallas_call | solution.py:310
  71.8 0.0 copy-start
  71.8 1.4 %copy.10 = f32[1,2,1,16,256]{4,3,2,1,0:T(8,128)} copy(f32[1,2,1,16,256]{4,3,2,1,0:T(8,128)} %get-tuple-element.10) | data formatting | bytes 65536
  73.2 0.0 copy-done
  73.2 0.6 copy.11
Async XLA Ops:
  71.8 1.4 %copy-start = (f32[1,2,1,16]{3,2,1,0:T(1,128)S(1)}, f32[1,2,1,16]{3,2,1,0:T(1,128)}, u32[]{:S(2)}) copy-start(f32[1,2,1,16]{3,2,1,0:T(1,128)} %get-tuple-element.5) | copy-start | bytes 388

commit v3 on v2

--- a/solution.py
+++ b/solution.py
@@ -16,7 +16,7 @@
 bf16, f32, i32 = jnp.bfloat16, jnp.float32, jnp.int32
 
 SPAN, SLOT, PLANE, TARGET, TOTAL, DOT = (16 * i for i in range(6))
-SPAN_Y, SPAN_X, SPAN_C, TARGET_C, SUM_C, RING = 96, 97, 100, 101, 102, 103
+SPAN_Y, SPAN_X, SPAN_C, TARGET_C, SUM_C, RING = 96, 97, 99, 101, 102, 103
 SEMAPHORES = 120
 
 
@@ -74,25 +74,31 @@
         pltpu.make_async_copy(orbitals.at[0, :, ga], slots.at[0, :, rows_of(ga)], local.at[2]),
         pltpu.make_async_copy(orbitals.at[0, :, 0], targets.at[0, :, rows_of(ga)], local.at[3]),
     ]
-    wide = pltpu.make_async_copy(spans.at[ka], span_wide, local.at[4])
-    wide.start()
+    wide = [
+        pltpu.make_async_copy(spans.at[q], span_wide.at[n], local.at[4 + n])
+        for n, q in enumerate((ka, lax.rem(ka + 8, 16)))
+    ]
+    for copy in wide:
+        copy.start()
     for copy in copies:
         copy.start()
 
     place = lax.broadcasted_iota(i32, (ROWS, 128), 0)
     lane = lax.broadcasted_iota(i32, (ROWS, 128), 1)
-    line = jnp.broadcast_to(owner[ka].astype(f32), (ROWS, ROWS))
-    line = jnp.where(lane[:, 0:ROWS] == place[:, 0:ROWS], line, 0.0)
-    owners = jnp.broadcast_to(jnp.sum(line, axis=1, keepdims=True), (ROWS, 128))
-    arrival = jnp.zeros((ROWS, 128), f32)
-    for earlier in range(ROWS - 1):
-        same = (owners == owners[earlier : earlier + 1]) & (place > earlier)
-        arrival = arrival + jnp.where(same, 1.0, 0.0)
     mine = lane == lax.rem(ga, 8) * ROWS + place
-    slot = jnp.where(mine, owners * 2.0 + arrival, 0.0)
-    slot_out[...] = jnp.sum(slot, axis=0, keepdims=True)
+    for n, q in enumerate((ka, lax.rem(ka + 8, 16))):
+        line = jnp.broadcast_to(owner[q].astype(f32), (ROWS, ROWS))
+        line = jnp.where(lane[:, 0:ROWS] == place[:, 0:ROWS], line, 0.0)
+        owners = jnp.broadcast_to(jnp.sum(line, axis=1, keepdims=True), (ROWS, 128))
+        arrival = jnp.zeros((ROWS, 128), f32)
+        for earlier in range(ROWS - 1):
+            same = (owners == owners[earlier : earlier + 1]) & (place > earlier)
+            arrival = arrival + jnp.where(same, 1.0, 0.0)
+        slot = jnp.where(mine, owners * 2.0 + arrival, 0.0)
+        slot_out[n] = jnp.sum(slot, axis=0, keepdims=True)
     slot_rows[ga] = slot_out[...]
-    wide.wait()
+    for copy in wide:
+        copy.wait()
     span_out[...] = span_wide[...].astype(bf16)
     span_block[ga] = span_out[...]
 
@@ -127,14 +133,16 @@
 
     arrived(send_span)
     arrived(send_slot)
-    block = span_block[...].reshape(N, 128).astype(f32)
-    weights[x, y, c, 0:128] = jnp.transpose(block).astype(bf16)
-    low = jnp.sum(slot_rows[0:8], axis=0)
-    high = jnp.sum(slot_rows[8:16], axis=0)
-    slot_line = jnp.concatenate([low, high], axis=1)
-    weights[x, y, c, 128:144] = jnp.broadcast_to(slot_line, (16, N)).astype(bf16)
-
-    span_y = remote(weights.at[x, y, c], weights.at[x, y, c], SPAN_Y, other_y)
+    parity, high = x % 2, x // 2
+    for n, row in enumerate((high, 1 - high)):
+        block = span_block[:, n].reshape(N, 128).astype(f32)
+        weights[parity, row, y, c, 0:128] = jnp.transpose(block).astype(bf16)
+        first = jnp.sum(slot_rows[0:8, n], axis=0)
+        second = jnp.sum(slot_rows[8:16, n], axis=0)
+        slot_line = jnp.concatenate([first, second], axis=1)
+        weights[parity, row, y, c, 128:144] = jnp.broadcast_to(slot_line, (16, N)).astype(bf16)
+
+    span_y = remote(weights.at[parity, :, y, c], weights.at[parity, :, y, c], SPAN_Y, other_y)
     span_y.start()
     for copy in copies:
         copy.wait()
@@ -154,18 +162,23 @@
         rings[-1].start()
         return rings[-1]
 
-    up1, up3, low4 = ring(0, upper, 1, back), ring(0, upper, 3, ahead), ring(0, lower, 4, other_y)
-    low1, low3, up4 = ring(0, lower, 1, back), ring(0, lower, 3, ahead), ring(0, upper, 4, other_y)
+    up1, up3 = ring(0, upper, 1, back), ring(0, upper, 3, ahead)
+    low4, up4 = ring(0, lower, 4, other_y), ring(0, upper, 4, other_y)
 
     over_ga(send_target)
 
+    def share(which, row, number, peer):
+        block = weights.at[which, row, :, c] if row is not None else weights.at[which, :, :, c]
+        copy = remote(block, block, number, peer)
+        copy.start()
+        return copy
+
     span_y.wait_recv()
-    span_x = [
-        remote(weights.at[x, :, c], weights.at[x, :, c], SPAN_X + n, along_x[i])
-        for n, i in enumerate((1, 3, 2))
-    ]
-    for copy in span_x:
-        copy.start()
+    span_ahead = share(parity, 0, SPAN_X, ahead)
+    span_back = share(parity, 1, SPAN_X + 1, back)
+    span_c = share(parity, None, SPAN_C, other_c)
+
+    low1, low3 = ring(0, lower, 1, back), ring(0, lower, 3, ahead)
 
     up1.wait_recv()
     up5 = ring(1, upper, 5, other_y)
@@ -174,25 +187,18 @@
     up3.wait_recv()
     up7 = ring(3, upper, 7, other_y)
     up2 = ring(1, upper, 2, back)
-    low3.wait_recv()
-    low2 = ring(3, lower, 2, ahead)
-
+
+    span_ahead.wait_recv()
+    span_back.wait_recv()
+    span_d = share(1 - parity, None, SPAN_C + 1, other_c)
     arrived(send_target)
     target_c = remote(targets.at[0], targets.at[1], TARGET_C, other_c)
     target_c.start()
-    for copy in span_x:
-        copy.wait_recv()
-    span_c = remote(weights.at[:, :, c], weights.at[:, :, c], SPAN_C, other_c)
-    span_c.start()
-
-    low5.wait_recv()
-    first6 = ring(5, quarters[0], 6, back)
-    low7.wait_recv()
-    second6 = ring(7, quarters[1], 6, ahead)
-    up5.wait_recv()
-    up6 = ring(5, upper, 6, back)
-
+
+    low3.wait_recv()
+    low2 = ring(3, lower, 2, ahead)
     span_c.wait_recv()
+    span_d.wait_recv()
 
     k_of_target = (ka, x * 4 + y * 2 + (1 - c))
 
@@ -204,7 +210,9 @@
         wanted = ((g2 // ROWS) * 2 + (g2 % ROWS - group) * 64).astype(f32)
         for t in range(2):
             q = q_index[k_of_target[t], partner_k]
-            table = weights[lax.div(q, 4), lax.rem(lax.div(q, 2), 2), lax.rem(q, 2)]
+            table = weights[
+                lax.rem(lax.div(q, 4), 2), lax.div(q, 8), lax.rem(lax.div(q, 2), 2), lax.rem(q, 2)
+            ]
             line = table[128:129].astype(f32)
             for arrival_number in range(2):
                 hot = (line == wanted + float(arrival_number)).astype(f32).astype(bf16)
@@ -215,7 +223,7 @@
                     part.astype(bf16)
                 )
 
-    def pairs(slot_numbers, first):
+    def pairs(slot_numbers, first, last=None):
         work = [(s, t) for s in slot_numbers for t in range(2)]
         for n, (s, t) in enumerate(work):
             h = dot(density(targets.at[t], slots.at[s]), dft[0]).astype(bf16)
@@ -230,7 +238,9 @@
             r = dot(dft[0], weighted[:, n * N : n * N + N]).astype(bf16)
             returned[n * N : n * N + N, 0:N] = r[0:N]
             returned[n * N : n * N + N, N : 2 * N] = r[N : 2 * N]
-        for n, (s, t) in enumerate(work):
+        for n, (s, t) in sorted(enumerate(work), key=lambda entry: -entry[1][1]):
+            if last is not None and t == 0 and n == 0:
+                last()
             potential = dot(returned[n * N : n * N + N, :], dft[1])
             partner_re, partner_im = slots[s, 0].astype(f32), slots[s, 1].astype(f32)
             v_re, v_im = potential[:, 0:N], potential[:, N : 2 * N]
@@ -243,11 +253,23 @@
                 acc[t, 0] += add_re
                 acc[t, 1] += add_im
 
+    to_other = remote(to_core, from_core, SUM_C, other_c)
+
+    def share_sum():
+        to_core[...] = acc[1].astype(bf16)
+        to_other.start()
+
     for s in range(8):
         expand(s)
     target_c.wait_recv()
     low1.wait_recv()
     pairs((0, 1), True)
+    low5.wait_recv()
+    first6 = ring(5, quarters[0], 6, back)
+    low7.wait_recv()
+    second6 = ring(7, quarters[1], 6, ahead)
+    up5.wait_recv()
+    up6 = ring(5, upper, 6, back)
     up4.wait_recv()
     pairs((3, 4), False)
     up2.wait_recv()
@@ -257,12 +279,9 @@
     first6.wait_recv()
     second6.wait_recv()
     up6.wait_recv()
-    pairs((7, 6), False)
-
-    to_core[...] = acc[1].astype(bf16)
-    sum_c = remote(to_core, from_core, SUM_C, other_c)
-    sum_c.start()
-    sum_c.wait_recv()
+    pairs((7, 6), False, share_sum)
+
+    to_other.wait_recv()
     to_ga[...] = (acc[0] + from_core[...].astype(f32)).astype(bf16)
 
     def send_total(i):
@@ -300,7 +319,8 @@
         def _(i):
             one(i).wait_send()
 
-    for copy in [span_y, *span_x, span_c, target_c, sum_c, *rings]:
+    spread = [span_y, span_ahead, span_back, span_c, span_d]
+    for copy in [*spread, target_c, to_other, *rings]:
         copy.wait_send()
 
 
@@ -320,12 +340,12 @@
             pltpu.VMEM((2, 16, ROWS, N), bf16),
             pltpu.VMEM((8, *plane), bf16),
             pltpu.VMEM((2, *plane), bf16),
-            pltpu.VMEM((ROWS, 128), f32),
-            pltpu.VMEM((GA, ROWS, 128), bf16),
-            pltpu.VMEM((ROWS, 128), bf16),
-            pltpu.VMEM((GA, 1, 128), f32),
-            pltpu.VMEM((1, 128), f32),
-            pltpu.VMEM((4, 2, 2, 144, N), bf16),
+            pltpu.VMEM((2, ROWS, 128), f32),
+            pltpu.VMEM((GA, 2, ROWS, 128), bf16),
+            pltpu.VMEM((2, ROWS, 128), bf16),
+            pltpu.VMEM((GA, 2, 1, 128), f32),
+            pltpu.VMEM((2, 1, 128), f32),
+            pltpu.VMEM((2, 2, 2, 2, 144, N), bf16),
             pltpu.VMEM((16, N, N), bf16),
             pltpu.VMEM((2 * N, 4 * N), bf16),
             pltpu.VMEM((2 * N, 4 * N), bf16),
@@ -339,7 +359,7 @@
             pltpu.VMEM((1, 128), f32),
             pltpu.SemaphoreType.DMA((SEMAPHORES,)),
             pltpu.SemaphoreType.DMA((SEMAPHORES,)),
-            pltpu.SemaphoreType.DMA((5,)),
+            pltpu.SemaphoreType.DMA((6,)),
         ],
         compiler_params=pltpu.CompilerParams(
             collective_id=0, has_side_effects=True, vmem_limit_bytes=60 * 2**20

time: 74 us -> 69.4 us (0.938)
  Pallas kernels: 71.1 us -> 66.5 us
    pallas_call x1, Pallas kernels: 71.1 us -> 66.5 us  [per_device(): pl.pallas_call(kernel, out_shape=(jax.ShapeDtypeStruct((1, 2, 1, ROWS, N)...]
where the time goes in v3:
time: 69.4 us; the launch traced here: 69.1 us
  Pallas kernels  66.5 us (96%)
  local copies, waits for them, and re-layouts  1.94 us (3%)
    pallas_call x1, Pallas kernels, per_device(): pl.pallas_call(kernel, out_shape=(jax.ShapeDtypeStruct((1, 2, 1, ROWS, N)...  66.5 us
    unnamed x4, local copies, waits for them, and re-layouts  1.94 us

profile of v3, /device:TPU:1, one launch (start us, length us, event | category | flops | bytes accessed | tf_op | source)
XLA Modules:
  0.0 69.1 jit_solution(13316964771643777289)
XLA Ops:
  0.6 66.5 %shard_map.68 = (f32[1,2,1,16,256]{4,3,2,1,0:T(8,128)}, f32[1,2,1,16]{3,2,1,0:T(1,128)}) custom-call(bf16[1,2,16,16,256]{4,3,2,1,0:T(8,128)(2,1)} %orbitals.1, f32[16,16,128]{2,1,0:T(8,128)} %spans.1, s32[16,1,16]{2,1,0:T(1,128)} %bitcast.4, s32[16,16]{1,0:T(8,128)} %q_index.1, bf16[2,512,512]{2,1,0:T(8,128)(2,1)} %constant.2.clone.tables), custom_call_target="tpu_custom_call" | custom-call | tf_op jit(solution)/shard_map/pallas_call | solution.py:330
  67.2 0.0 copy-start
  67.2 1.4 %copy.10 = f32[1,2,1,16,256]{4,3,2,1,0:T(8,128)} copy(f32[1,2,1,16,256]{4,3,2,1,0:T(8,128)} %get-tuple-element.10) | data formatting | bytes 65536
  68.5 0.0 copy-done
  68.5 0.6 copy.11
Async XLA Ops:
  67.2 1.4 %copy-start = (f32[1,2,1,16]{3,2,1,0:T(1,128)S(1)}, f32[1,2,1,16]{3,2,1,0:T(1,128)}, u32[]{:S(2)}) copy-start(f32[1,2,1,16]{3,2,1,0:T(1,128)} %get-tuple-element.5) | copy-start | bytes 388

commit v4 on v3

--- a/solution.py
+++ b/solution.py
@@ -127,6 +127,11 @@
         @pl.loop(1, GA)
         def _(i):
             one(i).wait_recv()
+
+    def sent(one):
+        @pl.loop(1, GA)
+        def _(i):
+            one(i).wait_send()
 
     over_ga(send_span, send_slot)
     over_ga(send_plane)
@@ -259,8 +264,8 @@
         to_core[...] = acc[1].astype(bf16)
         to_other.start()
 
-    for s in range(8):
-        expand(s)
+    expand(0)
+    expand(1)
     target_c.wait_recv()
     low1.wait_recv()
     pairs((0, 1), True)
@@ -270,6 +275,8 @@
     second6 = ring(7, quarters[1], 6, ahead)
     up5.wait_recv()
     up6 = ring(5, upper, 6, back)
+    for s in range(2, 8):
+        expand(s)
     up4.wait_recv()
     pairs((3, 4), False)
     up2.wait_recv()
@@ -290,6 +297,10 @@
 
     over_ga(send_total)
     from_ga[ga] = to_ga[:, rows_of(ga)]
+    for one in (send_span, send_slot, send_plane, send_target):
+        sent(one)
+    for copy in [span_y, span_ahead, span_back, span_c, span_d, target_c, to_other, *rings]:
+        copy.wait_send()
     arrived(send_total)
     total = jnp.sum(from_ga[...].astype(f32), axis=0) * (-1.0 / (16 * N * N))
     image[0, 0, 0] = total[0]
@@ -308,20 +319,13 @@
 
     over_ga(send_dots)
     dots[ga] = dot_out[...]
+    sent(send_total)
     arrived(send_dots)
     line = jnp.sum(dots[...], axis=0) * (1.0 / N)
     intersections[0, 0] = line[:, 0:16]
     intersections[0, 1] = line[:, 16:32]
 
-    for one in (send_span, send_slot, send_plane, send_target, send_total, send_dots):
-
-        @pl.loop(1, GA)
-        def _(i):
-            one(i).wait_send()
-
-    spread = [span_y, span_ahead, span_back, span_c, span_d]
-    for copy in [*spread, target_c, to_other, *rings]:
-        copy.wait_send()
+    sent(send_dots)
 
 
 def per_device(orbitals, kernel_spans, span_owner, q_index):

time: 69.4 us -> 69.3 us (level)
  no operation moved by 1% of the time
where the time goes in v4:
time: 69.3 us; the launch traced here: 69 us
  Pallas kernels  66.4 us (96%)
  local copies, waits for them, and re-layouts  1.94 us (3%)
    pallas_call x1, Pallas kernels, per_device(): pl.pallas_call(kernel, out_shape=(jax.ShapeDtypeStruct((1, 2, 1, ROWS, N)...  66.4 us
    unnamed x4, local copies, waits for them, and re-layouts  1.94 us

profile of v4, /device:TPU:1, one launch (start us, length us, event | category | flops | bytes accessed | tf_op | source)
XLA Modules:
  0.0 69.0 jit_solution(2671762608966785310)
XLA Ops:
  0.6 66.4 %shard_map.68 = (f32[1,2,1,16,256]{4,3,2,1,0:T(8,128)}, f32[1,2,1,16]{3,2,1,0:T(1,128)}) custom-call(bf16[1,2,16,16,256]{4,3,2,1,0:T(8,128)(2,1)} %orbitals.1, f32[16,16,128]{2,1,0:T(8,128)} %spans.1, s32[16,1,16]{2,1,0:T(1,128)} %bitcast.4, s32[16,16]{1,0:T(8,128)} %q_index.1, bf16[2,512,512]{2,1,0:T(8,128)(2,1)} %constant.2.clone.tables), custom_call_target="tpu_custom_call" | custom-call | tf_op jit(solution)/shard_map/pallas_call | solution.py:334
  67.1 0.0 copy-start
  67.1 1.4 %copy.10 = f32[1,2,1,16,256]{4,3,2,1,0:T(8,128)} copy(f32[1,2,1,16,256]{4,3,2,1,0:T(8,128)} %get-tuple-element.10) | data formatting | bytes 65536
  68.5 0.0 copy-done
  68.5 0.6 copy.11
Async XLA Ops:
  67.1 1.4 %copy-start = (f32[1,2,1,16]{3,2,1,0:T(1,128)S(1)}, f32[1,2,1,16]{3,2,1,0:T(1,128)}, u32[]{:S(2)}) copy-start(f32[1,2,1,16]{3,2,1,0:T(1,128)} %get-tuple-element.5) | copy-start | bytes 388

commit v5 on v4

--- a/solution.py
+++ b/solution.py
@@ -17,6 +17,7 @@
 
 SPAN, SLOT, PLANE, TARGET, TOTAL, DOT = (16 * i for i in range(6))
 SPAN_Y, SPAN_X, SPAN_C, TARGET_C, SUM_C, RING = 96, 97, 99, 101, 102, 103
+OWN_H, IMAGE_H = 118, 119
 SEMAPHORES = 120
 
 
@@ -44,7 +45,7 @@
 def kernel(
     orbitals, spans, owner, q_index, tables, image, intersections,
     dft, own, slots, targets, span_wide, span_block, span_out, slot_rows, slot_out, weights, kernels,
-    half, weighted, returned, acc, to_core, from_core, to_ga, from_ga, dots, dot_out,
+    half, weighted, returned, acc, to_core, from_core, to_ga, from_ga, partial, from_h, dots, dot_out,
     send, recv, local,
 ):
     ka, ga = lax.axis_index("ka"), lax.axis_index("ga")
@@ -53,6 +54,9 @@
     other_y = (x * 4 + (1 - y) * 2 + c, ga)
     other_c = (x * 4 + y * 2 + (1 - c), ga)
 
+    side, z = ga // 8, ga % 8
+    other_h = (ka, lax.rem(ga + 8, GA))
+
     def ga_peer(i):
         return (ka, lax.rem(ga + i, GA))
 
@@ -70,7 +74,7 @@
 
     copies = [
         pltpu.make_async_copy(tables, dft, local.at[0]),
-        pltpu.make_async_copy(orbitals.at[0], own, local.at[1]),
+        pltpu.make_async_copy(orbitals.at[0], own.at[side], local.at[1]),
         pltpu.make_async_copy(orbitals.at[0, :, ga], slots.at[0, :, rows_of(ga)], local.at[2]),
         pltpu.make_async_copy(orbitals.at[0, :, 0], targets.at[0, :, rows_of(ga)], local.at[3]),
     ]
@@ -275,6 +279,8 @@
     second6 = ring(7, quarters[1], 6, ahead)
     up5.wait_recv()
     up6 = ring(5, upper, 6, back)
+    own_h = remote(orbitals.at[0], own.at[side], OWN_H, other_h)
+    own_h.start()
     for s in range(2, 8):
         expand(s)
     up4.wait_recv()
@@ -289,26 +295,41 @@
     pairs((7, 6), False, share_sum)
 
     to_other.wait_recv()
-    to_ga[...] = (acc[0] + from_core[...].astype(f32)).astype(bf16)
+    total = acc[0] + from_core[...].astype(f32)
+    to_ga[...] = total.reshape(2, 2, 128, N).astype(bf16)
 
     def send_total(i):
-        peer = ga_peer(i)
-        return remote(to_ga.at[:, rows_of(peer[1])], from_ga.at[ga], TOTAL + i, peer)
-
-    over_ga(send_total)
-    from_ga[ga] = to_ga[:, rows_of(ga)]
+        place_z = lax.rem(z + i, 8)
+        peer = (ka, side * 8 + place_z)
+        return remote(to_ga.at[:, :, rows_of(place_z)], from_ga.at[z], TOTAL + i, peer)
+
+    @pl.loop(1, 8)
+    def _(i):
+        send_total(i).start()
+
+    from_ga[z] = to_ga[:, :, rows_of(z)]
     for one in (send_span, send_slot, send_plane, send_target):
         sent(one)
     for copy in [span_y, span_ahead, span_back, span_c, span_d, target_c, to_other, *rings]:
         copy.wait_send()
-    arrived(send_total)
+    own_h.wait()
+
+    @pl.loop(1, 8)
+    def _(i):
+        send_total(i).wait_recv()
+
     total = jnp.sum(from_ga[...].astype(f32), axis=0) * (-1.0 / (16 * N * N))
-    image[0, 0, 0] = total[0]
-    image[0, 1, 0] = total[1]
-
-    own_re, own_im = own[0].astype(f32), own[1].astype(f32)
-    re = jnp.sum(own_re * total[0][None] + own_im * total[1][None], axis=1)
-    im = jnp.sum(own_re * total[1][None] - own_im * total[0][None], axis=1)
+    partial[0] = total[:, 0]
+    partial[1] = total[:, 1]
+    image_h = remote(partial.at[1 - side], from_h, IMAGE_H, other_h)
+    image_h.start()
+
+    re, im = jnp.zeros((16, N), f32), jnp.zeros((16, N), f32)
+    for h in range(2):
+        own_re, own_im = own[h, 0].astype(f32), own[h, 1].astype(f32)
+        part_re, part_im = total[0, h][None], total[1, h][None]
+        re = re + jnp.sum(own_re * part_re + own_im * part_im, axis=1)
+        im = im + jnp.sum(own_re * part_im - own_im * part_re, axis=1)
     re = jnp.broadcast_to(jnp.sum(re, axis=1, keepdims=True), (16, 128))
     im = jnp.broadcast_to(jnp.sum(im, axis=1, keepdims=True), (16, 128))
     both = jnp.where(lane == place, re, 0.0) + jnp.where(lane == place + 16, im, 0.0)
@@ -319,7 +340,15 @@
 
     over_ga(send_dots)
     dots[ga] = dot_out[...]
-    sent(send_total)
+
+    @pl.loop(1, 8)
+    def _(i):
+        send_total(i).wait_send()
+
+    image_h.wait()
+    whole = partial[side] + from_h[...]
+    image[0, 0, 0] = whole[0]
+    image[0, 1, 0] = whole[1]
     arrived(send_dots)
     line = jnp.sum(dots[...], axis=0) * (1.0 / N)
     intersections[0, 0] = line[:, 0:16]
@@ -341,7 +370,7 @@
         out_specs=(vmem, vmem),
         scratch_shapes=[
             pltpu.VMEM((2, 2 * N, 2 * N), bf16),
-            pltpu.VMEM((2, 16, ROWS, N), bf16),
+            pltpu.VMEM((2, 2, 16, ROWS, N), bf16),
             pltpu.VMEM((8, *plane), bf16),
             pltpu.VMEM((2, *plane), bf16),
             pltpu.VMEM((2, ROWS, 128), f32),
@@ -357,8 +386,10 @@
             pltpu.VMEM((2, *plane), f32),
             pltpu.VMEM(plane, bf16),
             pltpu.VMEM(plane, bf16),
-            pltpu.VMEM(plane, bf16),
-            pltpu.VMEM((GA, 2, ROWS, N), bf16),
+            pltpu.VMEM((2, 2, 128, N), bf16),
+            pltpu.VMEM((8, 2, 2, ROWS, N), bf16),
+            pltpu.VMEM((2, 2, ROWS, N), f32),
+            pltpu.VMEM((2, ROWS, N), f32),
             pltpu.VMEM((GA, 1, 128), f32),
             pltpu.VMEM((1, 128), f32),
             pltpu.SemaphoreType.DMA((SEMAPHORES,)),

time: 69.3 us -> 69.2 us (level)
  no operation moved by 1% of the time
where the time goes in v5:
time: 69.2 us; the launch traced here: 68.9 us
  Pallas kernels  66.3 us (96%)
  local copies, waits for them, and re-layouts  1.94 us (3%)
    pallas_call x1, Pallas kernels, per_device(): pl.pallas_call(kernel, out_shape=(jax.ShapeDtypeStruct((1, 2, 1, ROWS, N)...  66.3 us
    unnamed x4, local copies, waits for them, and re-layouts  1.94 us

profile of v5, /device:TPU:1, one launch (start us, length us, event | category | flops | bytes accessed | tf_op | source)
XLA Modules:
  0.0 68.9 jit_solution(181364402811770021)
XLA Ops:
  0.6 66.3 %shard_map.68 = (f32[1,2,1,16,256]{4,3,2,1,0:T(8,128)}, f32[1,2,1,16]{3,2,1,0:T(1,128)}) custom-call(bf16[1,2,16,16,256]{4,3,2,1,0:T(8,128)(2,1)} %orbitals.1, f32[16,16,128]{2,1,0:T(8,128)} %spans.1, s32[16,1,16]{2,1,0:T(1,128)} %bitcast.4, s32[16,16]{1,0:T(8,128)} %q_index.1, bf16[2,512,512]{2,1,0:T(8,128)(2,1)} %constant.2.clone.tables), custom_call_target="tpu_custom_call" | custom-call | tf_op jit(solution)/shard_map/pallas_call | solution.py:363
  66.9 0.0 copy-start
  66.9 1.4 %copy.10 = f32[1,2,1,16,256]{4,3,2,1,0:T(8,128)} copy(f32[1,2,1,16,256]{4,3,2,1,0:T(8,128)} %get-tuple-element.10) | data formatting | bytes 65536
  68.3 0.0 copy-done
  68.3 0.6 copy.11
Async XLA Ops:
  66.9 1.4 %copy-start = (f32[1,2,1,16]{3,2,1,0:T(1,128)S(1)}, f32[1,2,1,16]{3,2,1,0:T(1,128)}, u32[]{:S(2)}) copy-start(f32[1,2,1,16]{3,2,1,0:T(1,128)} %get-tuple-element.5) | copy-start | bytes 388

commit v6 on v4

--- a/solution.py
+++ b/solution.py
@@ -228,8 +228,7 @@
                     part.astype(bf16)
                 )
 
-    def pairs(slot_numbers, first, last=None):
-        work = [(s, t) for s in slot_numbers for t in range(2)]
+    def pairs(work, first=False, between=None):
         for n, (s, t) in enumerate(work):
             h = dot(density(targets.at[t], slots.at[s]), dft[0]).astype(bf16)
             half[0:N, n * N : n * N + N] = h[:, 0:N]
@@ -239,13 +238,13 @@
             factor = kernels[s * 2 + t].astype(f32)
             weighted[0:N, n * N : n * N + N] = (spectrum[0:N] * factor).astype(bf16)
             weighted[N : 2 * N, n * N : n * N + N] = (spectrum[N : 2 * N] * factor).astype(bf16)
+        if between is not None:
+            between()
         for n in range(len(work)):
             r = dot(dft[0], weighted[:, n * N : n * N + N]).astype(bf16)
             returned[n * N : n * N + N, 0:N] = r[0:N]
             returned[n * N : n * N + N, N : 2 * N] = r[N : 2 * N]
-        for n, (s, t) in sorted(enumerate(work), key=lambda entry: -entry[1][1]):
-            if last is not None and t == 0 and n == 0:
-                last()
+        for n, (s, t) in enumerate(work):
             potential = dot(returned[n * N : n * N + N, :], dft[1])
             partner_re, partner_im = slots[s, 0].astype(f32), slots[s, 1].astype(f32)
             v_re, v_im = potential[:, 0:N], potential[:, N : 2 * N]
@@ -260,15 +259,31 @@
 
     to_other = remote(to_core, from_core, SUM_C, other_c)
 
-    def share_sum():
-        to_core[...] = acc[1].astype(bf16)
-        to_other.start()
+    def both(first, second):
+        return [(first, 0), (first, 1), (second, 0), (second, 1)]
+
+    def send_total(i):
+        peer = ga_peer(i)
+        return remote(to_ga.at[:, rows_of(peer[1])], from_ga.at[ga], TOTAL + i, peer)
+
+    def share_sum(giver):
+        @pl.when(c == giver)
+        def _():
+            to_core[...] = acc[1].astype(bf16)
+            to_other.start()
+
+    def take_sum(taker):
+        @pl.when(c == taker)
+        def _():
+            to_other.wait_recv()
+            to_ga[...] = (acc[0] + from_core[...].astype(f32)).astype(bf16)
+            over_ga(send_total)
 
     expand(0)
     expand(1)
     target_c.wait_recv()
     low1.wait_recv()
-    pairs((0, 1), True)
+    pairs(both(0, 1), True)
     low5.wait_recv()
     first6 = ring(5, quarters[0], 6, back)
     low7.wait_recv()
@@ -278,24 +293,20 @@
     for s in range(2, 8):
         expand(s)
     up4.wait_recv()
-    pairs((3, 4), False)
+    pairs(both(3, 4))
     up2.wait_recv()
     low2.wait_recv()
-    pairs((2, 5), False)
+    pairs(both(2, 5))
     up7.wait_recv()
     first6.wait_recv()
     second6.wait_recv()
     up6.wait_recv()
-    pairs((7, 6), False, share_sum)
-
-    to_other.wait_recv()
-    to_ga[...] = (acc[0] + from_core[...].astype(f32)).astype(bf16)
-
-    def send_total(i):
-        peer = ga_peer(i)
-        return remote(to_ga.at[:, rows_of(peer[1])], from_ga.at[ga], TOTAL + i, peer)
-
-    over_ga(send_total)
+    pairs([(7, c), (6, c)])
+    share_sum(1)
+    pairs([(7, 1 - c), (6, 1 - c)], between=lambda: take_sum(0))
+    share_sum(0)
+    take_sum(1)
+
     from_ga[ga] = to_ga[:, rows_of(ga)]
     for one in (send_span, send_slot, send_plane, send_target):
         sent(one)
@@ -311,8 +322,8 @@
     im = jnp.sum(own_re * total[1][None] - own_im * total[0][None], axis=1)
     re = jnp.broadcast_to(jnp.sum(re, axis=1, keepdims=True), (16, 128))
     im = jnp.broadcast_to(jnp.sum(im, axis=1, keepdims=True), (16, 128))
-    both = jnp.where(lane == place, re, 0.0) + jnp.where(lane == place + 16, im, 0.0)
-    dot_out[...] = jnp.sum(both, axis=0, keepdims=True)
+    line = jnp.where(lane == place, re, 0.0) + jnp.where(lane == place + 16, im, 0.0)
+    dot_out[...] = jnp.sum(line, axis=0, keepdims=True)
 
     def send_dots(i):
         return remote(dot_out, dots.at[ga], DOT + i, ga_peer(i))

time: 69.3 us -> 68.4 us (0.987)
  Pallas kernels: 66.4 us -> 65.5 us
    pallas_call x1, Pallas kernels: 66.4 us -> 65.5 us  [per_device(): pl.pallas_call(kernel, out_shape=(jax.ShapeDtypeStruct((1, 2, 1, ROWS, N)...]
where the time goes in v6:
time: 68.4 us; the launch traced here: 68.1 us
  Pallas kernels  65.5 us (96%)
  local copies, waits for them, and re-layouts  1.94 us (3%)
    pallas_call x1, Pallas kernels, per_device(): pl.pallas_call(kernel, out_shape=(jax.ShapeDtypeStruct((1, 2, 1, ROWS, N)...  65.5 us
    unnamed x4, local copies, waits for them, and re-layouts  1.94 us

profile of v6, /device:TPU:1, one launch (start us, length us, event | category | flops | bytes accessed | tf_op | source)
XLA Modules:
  0.0 68.1 jit_solution(8389410119776081100)
XLA Ops:
  0.6 65.5 %shard_map.68 = (f32[1,2,1,16,256]{4,3,2,1,0:T(8,128)}, f32[1,2,1,16]{3,2,1,0:T(1,128)}) custom-call(bf16[1,2,16,16,256]{4,3,2,1,0:T(8,128)(2,1)} %orbitals.1, f32[16,16,128]{2,1,0:T(8,128)} %spans.1, s32[16,1,16]{2,1,0:T(1,128)} %bitcast.4, s32[16,16]{1,0:T(8,128)} %q_index.1, bf16[2,512,512]{2,1,0:T(8,128)(2,1)} %constant.2.clone.tables), custom_call_target="tpu_custom_call" | custom-call | tf_op jit(solution)/shard_map/pallas_call | solution.py:345
  66.1 0.0 copy-start
  66.1 1.4 %copy.10 = f32[1,2,1,16,256]{4,3,2,1,0:T(8,128)} copy(f32[1,2,1,16,256]{4,3,2,1,0:T(8,128)} %get-tuple-element.10) | data formatting | bytes 65536
  67.5 0.0 copy-done
  67.5 0.6 copy.11
Async XLA Ops:
  66.1 1.4 %copy-start = (f32[1,2,1,16]{3,2,1,0:T(1,128)S(1)}, f32[1,2,1,16]{3,2,1,0:T(1,128)}, u32[]{:S(2)}) copy-start(f32[1,2,1,16]{3,2,1,0:T(1,128)} %get-tuple-element.5) | copy-start | bytes 388

commit v7 on v6

--- a/solution.py
+++ b/solution.py
@@ -283,13 +283,17 @@
     expand(1)
     target_c.wait_recv()
     low1.wait_recv()
-    pairs(both(0, 1), True)
-    low5.wait_recv()
-    first6 = ring(5, quarters[0], 6, back)
-    low7.wait_recv()
-    second6 = ring(7, quarters[1], 6, ahead)
-    up5.wait_recv()
-    up6 = ring(5, upper, 6, back)
+    last_relays = []
+
+    def relay():
+        low5.wait_recv()
+        last_relays.append(ring(5, quarters[0], 6, back))
+        low7.wait_recv()
+        last_relays.append(ring(7, quarters[1], 6, ahead))
+        up5.wait_recv()
+        last_relays.append(ring(5, upper, 6, back))
+
+    pairs(both(0, 1), True, relay)
     for s in range(2, 8):
         expand(s)
     up4.wait_recv()
@@ -298,9 +302,8 @@
     low2.wait_recv()
     pairs(both(2, 5))
     up7.wait_recv()
-    first6.wait_recv()
-    second6.wait_recv()
-    up6.wait_recv()
+    for copy in last_relays:
+        copy.wait_recv()
     pairs([(7, c), (6, c)])
     share_sum(1)
     pairs([(7, 1 - c), (6, 1 - c)], between=lambda: take_sum(0))

time: 68.4 us -> 69 us (level)
  no operation moved by 1% of the time
where the time goes in v7:
time: 69 us; the launch traced here: 68.7 us
  Pallas kernels  66.1 us (96%)
  local copies, waits for them, and re-layouts  1.94 us (3%)
    pallas_call x1, Pallas kernels, per_device(): pl.pallas_call(kernel, out_shape=(jax.ShapeDtypeStruct((1, 2, 1, ROWS, N)...  66.1 us
    unnamed x4, local copies, waits for them, and re-layouts  1.94 us

profile of v7, /device:TPU:1, one launch (start us, length us, event | category | flops | bytes accessed | tf_op | source)
XLA Modules:
  0.0 68.7 jit_solution(13366251436898557962)
XLA Ops:
  0.6 66.1 %shard_map.68 = (f32[1,2,1,16,256]{4,3,2,1,0:T(8,128)}, f32[1,2,1,16]{3,2,1,0:T(1,128)}) custom-call(bf16[1,2,16,16,256]{4,3,2,1,0:T(8,128)(2,1)} %orbitals.1, f32[16,16,128]{2,1,0:T(8,128)} %spans.1, s32[16,1,16]{2,1,0:T(1,128)} %bitcast.4, s32[16,16]{1,0:T(8,128)} %q_index.1, bf16[2,512,512]{2,1,0:T(8,128)(2,1)} %constant.2.clone.tables), custom_call_target="tpu_custom_call" | custom-call | tf_op jit(solution)/shard_map/pallas_call | solution.py:348
  66.7 0.0 copy-start
  66.7 1.4 %copy.10 = f32[1,2,1,16,256]{4,3,2,1,0:T(8,128)} copy(f32[1,2,1,16,256]{4,3,2,1,0:T(8,128)} %get-tuple-element.10) | data formatting | bytes 65536
  68.1 0.0 copy-done
  68.1 0.6 copy.11
Async XLA Ops:
  66.7 1.4 %copy-start = (f32[1,2,1,16]{3,2,1,0:T(1,128)S(1)}, f32[1,2,1,16]{3,2,1,0:T(1,128)}, u32[]{:S(2)}) copy-start(f32[1,2,1,16]{3,2,1,0:T(1,128)} %get-tuple-element.5) | copy-start | bytes 388
